TPU v7x, 1024 devices: a whole 4x8x16 slice. The times are simulated.
1024 devices in a mesh: row: 8 (over x, core), col: 128 (over z, y).
Axes of the slice: x: 4, y: 8, z: 16, core: 2. Of those that a mesh axis runs over, the one named last changes fastest.
Arguments:
- vectors: float32 [16384, 16384], P('row', 'col'), may hold values from -6 to 6
- reflectors: float32 [8, 256, 256, 128], P('row', 'col'), may hold values from -0.375 to 0.375
- wy_factors: float32 [8, 256, 128, 128], P('row', 'col'), may hold values from -1 to 3, as said below
- block_slots: int32 [8, 4, 4], P('row'), may hold values from 0 to 255, as said below
- offsets: int32 [8, 4, 3], P('row'), may hold values from 0 to 1792
Outputs:
- transformed: float32 [16384, 16384], P('row', 'col')
Inputs may be any that keep to these rules, and one draw needn't show every extreme that they name: `wy_factors`: upper triangular; diagonal entries between 1.2 and 2.8. `block_slots`: the entries of one row group are distinct; slot k of every group lies on the col index k // 2. The border entry of the last row group is not read.
All inputs are finite; a program needn't handle non-finite values.
Results may differ from a plain program's by a relative error of at most 0.00026.
Values sent between devices are 32-bit elements; how exact they have to be, the bound alone decides.
A program may use at most 32 MiB of HBM per device.

v0:
```python
import jax
import jax.numpy as jnp
from jax import lax
from jax.sharding import PartitionSpec as P


def spread(block, axis, source):
    block = jnp.where(lax.axis_index(axis) == source, block, jnp.zeros_like(block))
    return lax.psum(block, axis)


def shifted(block, axis, distance):
    devices = range(lax.axis_size(axis))
    route = [(i - distance, i) for i in devices if i - distance in devices]
    return lax.ppermute(block, axis, route)


def reflect(block, basis, factor):
    best = lax.Precision.HIGHEST
    coeffs = jnp.dot(basis.T, block, precision=best, preferred_element_type=jnp.float32)
    scaled = jnp.dot(factor, coeffs, precision=best, preferred_element_type=jnp.float32)
    return block - jnp.dot(basis, scaled, precision=best, preferred_element_type=jnp.float32)


def fetch_block(block_slots, reflectors, wy_factors, step_no, block_no):
    hold_count = reflectors.shape[1]
    slot_id = block_slots[0, step_no, block_no]
    local_slot = slot_id % hold_count
    root_col = slot_id // hold_count
    parcel = (
        lax.dynamic_index_in_dim(reflectors[0], local_slot, 0, False),
        lax.dynamic_index_in_dim(wy_factors[0], local_slot, 0, False),
    )
    return (spread(parcel[0], "col", root_col), spread(parcel[1], "col", root_col))


def advance(
    current, incoming, beneath, step_no, group_index, group_total_count, bases, factors, offsets
):
    edge_rows = beneath.shape[0]
    total_rows = current.shape[0]
    inner_count = offsets.shape[2]
    head = jnp.where(group_index > 0, incoming, current[:edge_rows])
    current = lax.dynamic_update_slice_in_dim(current, head, 0, 0)
    step_bases = lax.dynamic_index_in_dim(bases, step_no, 0, False)
    step_factors = lax.dynamic_index_in_dim(factors, step_no, 0, False)
    step_offsets = lax.dynamic_index_in_dim(offsets[0], step_no, 0, False)
    for block_no in range(inner_count):
        start = step_offsets[block_no]
        block = lax.dynamic_slice_in_dim(current, start, 2 * edge_rows, 0)
        block = reflect(block, step_bases[block_no], step_factors[block_no])
        current = lax.dynamic_update_slice_in_dim(current, block, start, 0)
    bottom = current[total_rows - edge_rows :]
    joined = reflect(
        jnp.concatenate([bottom, beneath], 0), step_bases[inner_count], step_factors[inner_count]
    )
    has_below = group_index < group_total_count - 1
    tail = jnp.where(has_below, joined[:edge_rows], bottom)
    current = lax.dynamic_update_slice_in_dim(current, tail, total_rows - edge_rows, 0)
    return (current, joined[edge_rows:])


def per_device(vectors, reflectors, wy_factors, block_slots, offsets):
    group_total_count = lax.axis_size("row")
    group_index = lax.axis_index("row")
    step_count = offsets.shape[1]
    inner_count = offsets.shape[2]
    edge_rows = reflectors.shape[3]
    column_count = vectors.shape[1]
    base_list = []
    factor_list = []
    for step_no in range(step_count):
        for block_no in range(inner_count + 1):
            basis, factor = fetch_block(block_slots, reflectors, wy_factors, step_no, block_no)
            base_list.append(basis)
            factor_list.append(factor)
    bases = jnp.stack(base_list).reshape((step_count, inner_count + 1) + base_list[0].shape)
    factors = jnp.stack(factor_list).reshape((step_count, inner_count + 1) + factor_list[0].shape)
    empty_rows = jnp.zeros((edge_rows, column_count), jnp.float32)
    current = vectors
    for step_no in range(step_count):
        beneath = shifted(current[:edge_rows], "row", -1)

        def take_turn(turn_no, carry, beneath=beneath, step_no=step_no):
            current, incoming = carry
            current, outgoing = lax.cond(
                group_index == turn_no,
                lambda operands: advance(
                    operands[0],
                    operands[1],
                    beneath,
                    step_no,
                    group_index,
                    group_total_count,
                    bases,
                    factors,
                    offsets,
                ),
                lambda operands: (operands[0], jnp.zeros_like(operands[1])),
                (current, incoming),
            )
            incoming = shifted(outgoing, "row", 1)
            return (current, incoming)

        current, incoming = lax.fori_loop(
            0, group_total_count - 1, take_turn, (current, empty_rows)
        )
        current = lax.cond(
            group_index == group_total_count - 1,
            lambda operands: advance(
                operands[0],
                operands[1],
                beneath,
                step_no,
                group_index,
                group_total_count,
                bases,
                factors,
                offsets,
            )[0],
            lambda operands: operands[0],
            (current, incoming),
        )
    return current


def solution(mesh):
    in_specs = (
        P("row", "col"),
        P("row", "col", None, None),
        P("row", "col", None, None),
        P("row", None, None),
        P("row", None, None),
    )
    out_specs = P("row", "col")
    return jax.shard_map(
        per_device, mesh=mesh, in_specs=in_specs, out_specs=out_specs, check_vma=False
    )
```

profile of v0, /device:TPU:31, one launch (start us, length us, event | category | flops | bytes accessed | tf_op | source)
XLA Modules:
  0.0 911.8 jit_solution(14855159491634816079)
XLA Ops:
  6.5 2.0 fusion.372
  49.3 2.2 select_bitcast_fusion.16
  55.2 2.6 collective-permute-start.4
  57.8 318.6 %all-reduce.3.cloned.1.call-done = (f32[1,256,128]{2,1,0:T(8,128)}, f32[1,256,128]{2,1,0:T(8,128)}, f32[1,256,128]{2,1,0:T(8,128)}, f32[1,256,128]{2,1,0:T(8,128...) async-done(((f32[1,256,128]{2,1,0:T(8,128)}, ...) | async-done | bytes 3145744 | tf_op jit(solution)/shard_map/psum | solution.py:9
  391.1 150.9 %while.84 = (s32[]{:T(128)}, f32[2048,128]{0,1:T(8,128)S(1)}, f32[128,128]{0,1:T(8,128)S(1)}, s32[]{:T(128)}, s32[1,4,3]{1,0,2:T(1,128)S(1)}, /*index=5*/f32[4,4...) while((s32[]{:T(128)}, f32[2048,128]{0,1:T(8,128)S(1)}, ...), condition=%wide.region_35.36_spmd, body=%wide.region_32.35_spmd.sunk | while | flops 503545856 | bytes 5636497 | solution.py:105
  391.1 1.3 collective-permute-start
  392.4 9.4 %collective-permute-done = f32[128,128]{0,1:T(8,128)S(1)} collective-permute-done((f32[128,128]{0,1:T(8,128)S(1)}, f32[128,128]{0,1:T(8,128)S(1)}, u32[]{:S(2)}, u32[]{:S(2)}) %collective-permute-start) | collective-permute-done | bytes 65568 | tf_op jit(solution)/shard_map/while/body/eval_jaxpr/ppermute | solution.py:15
  403.1 4.3 collective-permute-done
  408.6 4.3 collective-permute-done
  412.9 1.3 collective-permute-start
  414.2 4.3 collective-permute-done
  419.8 4.3 collective-permute-done
  425.4 4.3 collective-permute-done
  429.7 1.3 collective-permute-start
  431.0 111.0 %collective-permute-done = f32[128,128]{0,1:T(8,128)S(1)} collective-permute-done((f32[128,128]{0,1:T(8,128)S(1)}, f32[128,128]{0,1:T(8,128)S(1)}, u32[]{:S(2)}, u32[]{:S(2)}) %collective-permute-start) | collective-permute-done | bytes 65568 | tf_op jit(solution)/shard_map/while/body/eval_jaxpr/ppermute | solution.py:15
  542.0 17.1 %conditional.8 = (f32[2048,128]{0,1:T(8,128)S(1)}) conditional(s32[]{:T(128)} %convert_element_type.34, f32[2048,128]{0,1:T(8,128)S(1)} %get-tuple-element.769, (s32[]{:T(128)}, f32[2048,128]{0,1:T(8,128)S(1)}, f32[128,128]{0,1:T(8,128)S(1)}, s32[1,4,3]{1,0,2:T(1,128)S(1)}, f32[4,4,256,128]{3,2,1,0:T(8,128)S(1)}, ...), branch_computations={%region_36.37_spmd, %region_37.38_spmd} | conditional | flops 503513088 | bytes 5177534 | solution.py:108
  546.2 1.3 dynamic_update_slice.86
  551.1 1.3 dynamic_update_slice.87
  556.0 1.3 dynamic_update_slice.88
  559.1 1.5 collective-permute-start.5
  561.3 95.7 %while.85 = (s32[]{:T(128)}, f32[2048,128]{0,1:T(8,128)S(1)}, f32[128,128]{0,1:T(8,128)S(1)}, s32[]{:T(128)}, s32[1,4,3]{1,0,2:T(1,128)S(1)}, /*index=5*/f32[4,4...) while((s32[]{:T(128)}, f32[2048,128]{0,1:T(8,128)S(1)}, ...), condition=%wide.region_41.42_spmd, body=%wide.region_38.41_spmd.sunk | while | flops 503545856 | bytes 5636497 | solution.py:105
  561.3 1.3 collective-permute-start.1
  562.6 1.8 collective-permute-done.1
  565.7 4.1 collective-permute-done.1
  569.9 1.3 collective-permute-start.1
  571.2 4.3 collective-permute-done.1
  576.7 4.3 collective-permute-done.1
  582.3 4.3 collective-permute-done.1
  586.6 1.3 collective-permute-start.1
  587.9 4.3 collective-permute-done.1
  593.5 63.5 %collective-permute-done.1 = f32[128,128]{0,1:T(8,128)S(1)} collective-permute-done((f32[128,128]{0,1:T(8,128)S(1)}, f32[128,128]{0,1:T(8,128)S(1)}, u32[]{:S(2)}, u32[]{:S(2)}) %collective-permute-start.1) | collective-permute-done | bytes 65568 | tf_op jit(solution)/shard_map/while/body/eval_jaxpr/ppermute | solution.py:15
  657.0 17.1 %conditional.9 = (f32[2048,128]{0,1:T(8,128)S(1)}) conditional(s32[]{:T(128)} %convert_element_type.34, f32[2048,128]{0,1:T(8,128)S(1)} %get-tuple-element.771, (s32[]{:T(128)}, f32[2048,128]{0,1:T(8,128)S(1)}, f32[128,128]{0,1:T(8,128)S(1)}, s32[1,4,3]{1,0,2:T(1,128)S(1)}, f32[4,4,256,128]{3,2,1,0:T(8,128)S(1)}, ...), branch_computations={%region_42.43_spmd, %region_43.44_spmd} | conditional | flops 503513088 | bytes 5177534 | solution.py:108
  661.3 1.3 dynamic_update_slice.96
  666.2 1.3 dynamic_update_slice.97
  671.1 1.3 dynamic_update_slice.98
  674.1 1.3 collective-permute-start.6
  676.3 95.3 %while.86 = (s32[]{:T(128)}, f32[2048,128]{0,1:T(8,128)S(1)}, f32[128,128]{0,1:T(8,128)S(1)}, s32[]{:T(128)}, s32[1,4,3]{1,0,2:T(1,128)S(1)}, /*index=5*/f32[4,4...) while((s32[]{:T(128)}, f32[2048,128]{0,1:T(8,128)S(1)}, ...), condition=%wide.region_47.48_spmd, body=%wide.region_44.47_spmd.sunk | while | flops 503545856 | bytes 5636497 | solution.py:105
  676.4 1.3 collective-permute-start.2
  677.7 1.8 collective-permute-done.2
  679.5 1.3 collective-permute-start.2
  680.8 4.1 collective-permute-done.2
  684.9 1.3 collective-permute-start.2
  686.2 4.3 collective-permute-done.2
  691.8 4.3 collective-permute-done.2
  697.4 4.3 collective-permute-done.2
  703.0 4.3 collective-permute-done.2
  708.6 63.1 %collective-permute-done.2 = f32[128,128]{0,1:T(8,128)S(1)} collective-permute-done((f32[128,128]{0,1:T(8,128)S(1)}, f32[128,128]{0,1:T(8,128)S(1)}, u32[]{:S(2)}, u32[]{:S(2)}) %collective-permute-start.2) | collective-permute-done | bytes 65568 | tf_op jit(solution)/shard_map/while/body/eval_jaxpr/ppermute | solution.py:15
  771.7 16.9 %conditional.10 = (f32[2048,128]{0,1:T(8,128)S(1)}) conditional(s32[]{:T(128)} %convert_element_type.34, f32[2048,128]{0,1:T(8,128)S(1)} %get-tuple-element.773, (s32[]{:T(128)}, f32[2048,128]{0,1:T(8,128)S(1)}, f32[128,128]{0,1:T(8,128)S(1)}, s32[1,4,3]{1,0,2:T(1,128)S(1)}, f32[4,4,256,128]{3,2,1,0:T(8,128)S(1)}, ...), branch_computations={%region_48.49_spmd, %region_49.50_spmd} | conditional | flops 503513088 | bytes 5177534 | solution.py:108
  775.9 1.3 dynamic_update_slice.106
  785.6 1.3 dynamic_update_slice.108
  788.6 1.3 collective-permute-start.7
  790.8 96.0 %while.87 = (s32[]{:T(128)}, f32[2048,128]{0,1:T(8,128)S(1)}, f32[128,128]{0,1:T(8,128)S(1)}, s32[]{:T(128)}, s32[1,4,3]{1,0,2:T(1,128)S(1)}, /*index=5*/f32[4,4...) while((s32[]{:T(128)}, f32[2048,128]{0,1:T(8,128)S(1)}, ...), condition=%wide.region_53.54_spmd, body=%wide.region_50.53_spmd.sunk | while | flops 503545856 | bytes 5636497 | solution.py:105
  790.8 1.3 collective-permute-start.3
  792.1 1.8 collective-permute-done.3
  795.3 4.1 collective-permute-done.3
  800.7 4.3 collective-permute-done.3
  806.3 4.3 collective-permute-done.3
  811.9 4.3 collective-permute-done.3
  817.4 4.3 collective-permute-done.3
  823.0 63.7 %collective-permute-done.3 = f32[128,128]{0,1:T(8,128)S(1)} collective-permute-done((f32[128,128]{0,1:T(8,128)S(1)}, f32[128,128]{0,1:T(8,128)S(1)}, u32[]{:S(2)}, u32[]{:S(2)}) %collective-permute-start.3) | collective-permute-done | bytes 65568 | tf_op jit(solution)/shard_map/while/body/eval_jaxpr/ppermute | solution.py:15
  886.8 16.9 %conditional.11 = (f32[2048,128]{0,1:T(8,128)S(1)}) conditional(s32[]{:T(128)} %convert_element_type.34, f32[2048,128]{0,1:T(8,128)S(1)} %get-tuple-element.775, (s32[]{:T(128)}, f32[2048,128]{0,1:T(8,128)S(1)}, f32[128,128]{0,1:T(8,128)S(1)}, s32[1,4,3]{1,0,2:T(1,128)S(1)}, f32[4,4,256,128]{3,2,1,0:T(8,128)S(1)}, ...), branch_computations={%region_54.55_spmd, %region_55.56_spmd} | conditional | flops 503513088 | bytes 5177534 | solution.py:108
  891.1 1.3 dynamic_update_slice.116
  896.0 1.3 dynamic_update_slice.117
  903.7 1.3 copy.10
  (234 shorter events, 76.0 us)
Async XLA Ops:
  6.5 44.9 %copy-start.1 = (f32[1,2,256,128]{3,2,1,0:T(8,128)S(1)}, f32[1,2,256,128]{3,2,1,0:T(8,128)}, u32[]{:S(2)}) copy-start(f32[1,2,256,128]{3,2,1,0:T(8,128)} %param.30) | copy-start | bytes 786436
  6.5 369.9 %all-reduce.3.cloned.1.call-start = ((), (), s32[]{:S(2)}) async-start(), calls=%async_computation | async-start | bytes 6291456 | tf_op jit(solution)/shard_map/psum | solution.py:9
  19.2 33.4 %copy-start.2 = (f32[1,2,128,128]{3,2,1,0:T(8,128)S(1)}, f32[1,2,128,128]{3,2,1,0:T(8,128)}, u32[]{:S(2)}) copy-start(f32[1,2,128,128]{3,2,1,0:T(8,128)} %param.31) | copy-start | bytes 393220
  53.3 1.6 copy-start.3
  55.2 334.9 %collective-permute-start.4 = (f32[128,128]{0,1:T(8,128)S(1)}, f32[128,128]{0,1:T(8,128)S(1)}, u32[]{:S(2)}, u32[]{:S(2)}) collective-permute-start(f32[128,128]{0,1:T(8,128)S(1)} %slice.656), channel_id=1, source_target_pairs={{128,0},{256,128},{384,256},{512,384},{640,512},{768,640},{896,768... | collective-permute-start | bytes 196616 | tf_op jit(solution)/shard_map/ppermute | solution.py:15
  376.4 13.2 %copy-start.21 = (f32[1,128,128]{2,1,0:T(8,128)S(1)}, f32[1,128,128]{2,1,0:T(8,128)}, u32[]{:S(2)}) copy-start(f32[1,128,128]{2,1,0:T(8,128)} %get-tuple-element.880) | copy-start | bytes 196612
  376.4 13.2 %copy-start.19 = (f32[1,256,128]{2,1,0:T(8,128)S(1)}, f32[1,256,128]{2,1,0:T(8,128)}, u32[]{:S(2)}) copy-start(f32[1,256,128]{2,1,0:T(8,128)} %get-tuple-element.851) | copy-start | bytes 393220
  376.4 13.2 %copy-start.18 = (f32[1,256,128]{2,1,0:T(8,128)S(1)}, f32[1,256,128]{2,1,0:T(8,128)}, u32[]{:S(2)}) copy-start(f32[1,256,128]{2,1,0:T(8,128)} %get-tuple-element.852) | copy-start | bytes 393220
  376.4 13.3 %copy-start.17 = (f32[1,256,128]{2,1,0:T(8,128)S(1)}, f32[1,256,128]{2,1,0:T(8,128)}, u32[]{:S(2)}) copy-start(f32[1,256,128]{2,1,0:T(8,128)} %get-tuple-element.853) | copy-start | bytes 393220
  376.4 13.3 %copy-start.16 = (f32[1,256,128]{2,1,0:T(8,128)S(1)}, f32[1,256,128]{2,1,0:T(8,128)}, u32[]{:S(2)}) copy-start(f32[1,256,128]{2,1,0:T(8,128)} %get-tuple-element.854) | copy-start | bytes 393220
  376.4 13.3 %copy-start.15 = (f32[1,256,128]{2,1,0:T(8,128)S(1)}, f32[1,256,128]{2,1,0:T(8,128)}, u32[]{:S(2)}) copy-start(f32[1,256,128]{2,1,0:T(8,128)} %get-tuple-element.855) | copy-start | bytes 393220
  376.4 13.3 %copy-start.14 = (f32[1,256,128]{2,1,0:T(8,128)S(1)}, f32[1,256,128]{2,1,0:T(8,128)}, u32[]{:S(2)}) copy-start(f32[1,256,128]{2,1,0:T(8,128)} %get-tuple-element.856) | copy-start | bytes 393220
  376.4 13.4 %copy-start.13 = (f32[1,256,128]{2,1,0:T(8,128)S(1)}, f32[1,256,128]{2,1,0:T(8,128)}, u32[]{:S(2)}) copy-start(f32[1,256,128]{2,1,0:T(8,128)} %get-tuple-element.857) | copy-start | bytes 393220
  376.4 13.4 %copy-start.12 = (f32[1,256,128]{2,1,0:T(8,128)S(1)}, f32[1,256,128]{2,1,0:T(8,128)}, u32[]{:S(2)}) copy-start(f32[1,256,128]{2,1,0:T(8,128)} %get-tuple-element.858) | copy-start | bytes 393220
  377.4 12.5 %copy-start.11 = (f32[1,256,128]{2,1,0:T(8,128)S(1)}, f32[1,256,128]{2,1,0:T(8,128)}, u32[]{:S(2)}) copy-start(f32[1,256,128]{2,1,0:T(8,128)} %get-tuple-element.859) | copy-start | bytes 393220
  378.3 11.5 %copy-start.10 = (f32[1,256,128]{2,1,0:T(8,128)S(1)}, f32[1,256,128]{2,1,0:T(8,128)}, u32[]{:S(2)}) copy-start(f32[1,256,128]{2,1,0:T(8,128)} %get-tuple-element.860) | copy-start | bytes 393220
  380.1 9.8 %copy-start.9 = (f32[1,256,128]{2,1,0:T(8,128)S(1)}, f32[1,256,128]{2,1,0:T(8,128)}, u32[]{:S(2)}) copy-start(f32[1,256,128]{2,1,0:T(8,128)} %get-tuple-element.861) | copy-start | bytes 393220
  381.8 8.1 copy-start.8
  383.5 6.4 copy-start.7
  385.2 4.7 copy-start.6
  387.0 3.0 copy-start.5
  388.7 1.3 copy-start.20
  389.6 1.5 copy-start.4
  390.1 1.0 copy-start
  391.1 10.7 %collective-permute-start = (f32[128,128]{0,1:T(8,128)S(1)}, f32[128,128]{0,1:T(8,128)S(1)}, u32[]{:S(2)}, u32[]{:S(2)}) collective-permute-start(f32[128,128]{0,1:T(8,128)S(1)} %get-tuple-element.1143), channel_id=1, source_target_pairs={{0,128},{128,256},{256,384},{384,512},{512,640},{640,768},{768,896... | collective-permute-start | bytes 196616 | tf_op jit(solution)/shard_map/while/body/eval_jaxpr/ppermute | solution.py:15
  401.8 5.6 collective-permute-start
  407.3 5.6 collective-permute-start
  412.9 5.6 collective-permute-start
  418.5 5.6 collective-permute-start
  424.1 5.6 collective-permute-start
  429.7 112.3 %collective-permute-start = (f32[128,128]{0,1:T(8,128)S(1)}, f32[128,128]{0,1:T(8,128)S(1)}, u32[]{:S(2)}, u32[]{:S(2)}) collective-permute-start(f32[128,128]{0,1:T(8,128)S(1)} %get-tuple-element.1143), channel_id=1, source_target_pairs={{0,128},{128,256},{256,384},{384,512},{512,640},{640,768},{768,896... | collective-permute-start | bytes 196616 | tf_op jit(solution)/shard_map/while/body/eval_jaxpr/ppermute | solution.py:15
  559.1 2.2 collective-permute-start.5
  561.3 3.1 collective-permute-start.1
  564.4 5.4 collective-permute-start.1
  569.9 5.6 collective-permute-start.1
  575.5 5.6 collective-permute-start.1
  581.0 5.6 collective-permute-start.1
  586.6 5.6 collective-permute-start.1
  592.2 64.8 %collective-permute-start.1 = (f32[128,128]{0,1:T(8,128)S(1)}, f32[128,128]{0,1:T(8,128)S(1)}, u32[]{:S(2)}, u32[]{:S(2)}) collective-permute-start(f32[128,128]{0,1:T(8,128)S(1)} %get-tuple-element.1153), channel_id=1, source_target_pairs={{0,128},{128,256},{256,384},{384,512},{512,640},{640,768},{768,896... | collective-permute-start | bytes 196616 | tf_op jit(solution)/shard_map/while/body/eval_jaxpr/ppermute | solution.py:15
  674.1 2.2 collective-permute-start.6
  676.4 3.1 collective-permute-start.2
  679.5 5.4 collective-permute-start.2
  684.9 5.6 collective-permute-start.2
  690.5 5.6 collective-permute-start.2
  696.1 5.6 collective-permute-start.2
  701.7 5.6 collective-permute-start.2
  707.3 64.4 %collective-permute-start.2 = (f32[128,128]{0,1:T(8,128)S(1)}, f32[128,128]{0,1:T(8,128)S(1)}, u32[]{:S(2)}, u32[]{:S(2)}) collective-permute-start(f32[128,128]{0,1:T(8,128)S(1)} %get-tuple-element.1163), channel_id=1, source_target_pairs={{0,128},{128,256},{256,384},{384,512},{512,640},{640,768},{768,896... | collective-permute-start | bytes 196616 | tf_op jit(solution)/shard_map/while/body/eval_jaxpr/ppermute | solution.py:15
  788.6 2.2 collective-permute-start.7
  790.8 3.1 collective-permute-start.3
  794.0 5.4 collective-permute-start.3
  799.4 5.6 collective-permute-start.3
  805.0 5.6 collective-permute-start.3
  810.6 5.6 collective-permute-start.3
  816.2 5.6 collective-permute-start.3
  821.7 65.0 %collective-permute-start.3 = (f32[128,128]{0,1:T(8,128)S(1)}, f32[128,128]{0,1:T(8,128)S(1)}, u32[]{:S(2)}, u32[]{:S(2)}) collective-permute-start(f32[128,128]{0,1:T(8,128)S(1)} %get-tuple-element.1173), channel_id=1, source_target_pairs={{0,128},{128,256},{256,384},{384,512},{512,640},{640,768},{768,896... | collective-permute-start | bytes 196616 | tf_op jit(solution)/shard_map/while/body/eval_jaxpr/ppermute | solution.py:15
Sparse Core Ops, SparseCore 0:
  54.4 321.9 all-reduce.2
where the time goes:
time: 915 us; the launch traced here: 912 us
  waiting for transfers between devices  723 us (79%)
  between operations  54.6 us (6%)
  starting transfers between devices  42.5 us (5%)
  local copies, waits for them, and re-layouts  36.5 us (4%)
  matrix products  27.1 us (3%)
  loops' own time  23.4 us (3%)
    ppermute x32, waiting for transfers between devices, shifted(): return lax.ppermute(block, axis, route)  404 us
    psum x1, waiting for transfers between devices, spread(): return lax.psum(block, axis)  319 us
    ppermute x32, starting transfers between devices, shifted(): return lax.ppermute(block, axis, route)  42.5 us
    another operation x4, loops' own time, per_device(): lax.cond(group_index == group_total_count - 1, lambda operands: advance(o...  23 us
  transfers between devices with their start and end apart: 33, of which 32 were waited for; matrix products, arithmetic and copies ran while one was open for 1% of the time, Pallas kernels for 0%

commit v1 on v0

v1 whole, which is shorter than its diff:
```python
import functools

import jax
import jax.numpy as jnp
from jax import lax
from jax.experimental import pallas as pl
from jax.experimental.pallas import tpu as pltpu
from jax.sharding import PartitionSpec as P

MESH = pl.DeviceIdType.MESH
F32 = jnp.float32
BF16 = jnp.bfloat16
NY = 8
T = 4
PIECES = T * T
REACH = 896

TILE = [(dz, dy) for dz in (-1, 0, 1, 2) for dy in (-1, 0, 1, 2)]
NEAR = [(1, 0), (-1, 0), (2, 0), (-2, 0), (0, 1), (0, -1), (0, 2), (0, -2)]


def split(x):
    high = x.astype(BF16)
    return high, (x - high.astype(F32)).astype(BF16)


def mul(a, b):
    (ah, al), (bh, bl) = a, b
    dot = functools.partial(jnp.dot, preferred_element_type=F32)
    return dot(ah, bh) + (dot(ah, bl) + dot(al, bh))


def kernel(
    nz, groups, steps, inner,
    slots, offs, vec, refl, wy, out,
    got_v, got_t, mine, far, full, ident, shift_x, shift_e, head, beneath, down, delta,
    load_sem, s1, r1, s2, r2, s3, r3, s4, r4, s5, r5, sh, rh,
):
    blocks_step = inner + 1
    blocks = steps * blocks_step
    nzh, nyh = nz // T, NY // T
    nfar = nzh * nyh
    share = blocks // nfar
    group = lax.axis_index("row")
    col = lax.axis_index("col")
    z, y = col // NY, col % NY
    zl, yl, zh, yh = z % T, y % T, z // T, y // T
    f_me = zh * nyh + yh
    p_me = zl * T + yl

    def at(dz, dy):
        return {"col": ((z + dz + nz) % nz) * NY + (y + dy + NY) % NY}

    def row(d):
        return {"row": (group + d + groups) % groups}

    def send(src, dst, ssem, rsem, dev):
        return pltpu.make_async_remote_copy(
            src_ref=src, dst_ref=dst, send_sem=ssem, recv_sem=rsem, device_id=dev, device_id_type=MESH
        )

    fars = [(a, b) for a in range(nzh) for b in range(nyh) if (a, b) != (0, 0)]

    load = pltpu.make_async_copy(vec, out, load_sem.at[0])
    load.start()

    greet = {(-dz, -dy) for dz, dy in TILE} | set(NEAR)
    greet = {(dz % nz, dy % NY) for dz, dy in greet} | {(T * a, T * b) for a, b in fars}
    greet = sorted(greet - {(0, 0)})
    barrier = pltpu.get_barrier_semaphore()
    for dz, dy in greet:
        pl.semaphore_signal(barrier, inc=1, device_id=at(dz, dy), device_id_type=MESH)
    for d in (1, -1):
        pl.semaphore_signal(barrier, inc=1, device_id=row(d), device_id_type=MESH)
    pl.semaphore_wait(barrier, len(greet) + 2)

    first, own = [], []
    vr = got_v.shape[2]
    tr = got_t.shape[2]
    for k, (dz, dy) in enumerate(TILE):
        p = ((z + dz + nz) % T) * T + (y + dy + NY) % T
        src_v = refl.at[0, :, pl.ds(pl.multiple_of(p * vr, vr), vr)]
        src_t = wy.at[0, :, pl.ds(pl.multiple_of(p * tr, tr), tr)]
        if (dz, dy) == (0, 0):
            own = [
                pltpu.make_async_copy(src_v, got_v.at[k], load_sem.at[1]),
                pltpu.make_async_copy(src_t, got_t.at[k], load_sem.at[2]),
            ]
        else:
            first += [
                send(src_v, got_v.at[k], s1.at[k], r1.at[k], at(dz, dy)),
                send(src_t, got_t.at[k], s1.at[k + PIECES], r1.at[k + PIECES], at(dz, dy)),
            ]
    for c in first + own:
        c.start()

    shift_x[...] = jnp.zeros_like(shift_x)
    shift_e[...] = jnp.zeros_like(shift_e)
    for c in own:
        c.wait()
    for c in first:
        c.wait_recv()

    for b in range(blocks):
        slot = slots[0, b // blocks_step, b % blocks_step]
        root = slot // 2
        az = (z - root // NY + nz + 1) % nz
        ay = (y - root % NY + NY + 1) % NY
        here = jnp.logical_and(az < T, ay < T)
        k = jnp.minimum(az, T - 1) * T + jnp.minimum(ay, T - 1)
        half = slot % 2
        mine[b, 0:vr] = jnp.where(here, got_v[k, half], 0.0)
        mine[b, vr : vr + tr] = jnp.where(here, got_t[k, half], 0.0)
    second = []
    for a, b in fars:
        k = a * nyh + b
        dest = ((zh + a) % nzh) * nyh + (yh + b) % nyh
        second.append(send(mine.at[pl.ds(dest * share, share)], far.at[k], s2.at[k], r2.at[k], at(T * a, T * b)))
    for c in second:
        c.start()
    total = mine[pl.ds(f_me * share, share)]
    for c in second:
        c.wait_recv()
    for k in range(1, nfar):
        total = total + far[k]
    full[pl.ds(f_me * share, share), zl, yl] = total

    third = []
    for a, b in fars:
        k = a * nyh + b
        shard = full.at[pl.ds(f_me * share, share), zl, yl]
        third.append(send(shard, shard, s3.at[k], r3.at[k], at(T * a, T * b)))
    for c in third:
        c.start()
    for c in third:
        c.wait_recv()

    half = blocks_step // 2

    def near(step, turn):
        base = step * blocks_step
        sends, recvs = [], []
        s, r = (s4, r4) if turn == 0 else (s5, r5)
        for i, (dz, dy) in enumerate(NEAR):
            along_z = dy == 0
            lo = base + (0 if along_z == (turn == 0) else half)
            n = half
            if (dz, dy) in ((2, 0), (0, 2)):
                n = half // 2
            if (dz, dy) in ((-2, 0), (0, -2)):
                lo, n = lo + half // 2, half - half // 2
            if turn == 0:
                ref = full.at[pl.ds(lo, n), zl, yl]
            elif along_z:
                ref = full.at[pl.ds(lo, n), zl]
            else:
                ref = full.at[pl.ds(lo, n), :, yl]
            j = step * len(NEAR) + i
            sends.append(send(ref, ref, s.at[j], r.at[j], at(dz, dy)))
        return sends

    fourth = [near(s, 0) for s in range(steps)]
    fifth = [near(s, 1) for s in range(steps)]
    for cs in fourth:
        for c in cs:
            c.start()
    load.wait()
    for s in range(steps):
        for c in fourth[s]:
            c.wait_recv()
        for c in fifth[s]:
            c.start()

    rows = out.shape[0]
    edge = head.shape[1]
    tall = 2 * edge
    has_below = group < groups - 1
    eye = (
        lax.broadcasted_iota(jnp.int32, (edge, edge), 0) == lax.broadcasted_iota(jnp.int32, (edge, edge), 1)
    ).astype(F32)
    halo = []

    def block(b):
        basis = full[b, :, :, 0:vr].reshape(tall, edge)
        factor = full[b, :, :, vr : vr + tr].reshape(edge, edge)
        return split(basis.T), split(factor), split(basis)

    def apply(ops, x):
        w = mul(ops[0], split(x))
        return mul(ops[2], split(mul(ops[1], split(w))))

    for s in range(steps):
        up = send(head.at[s], beneath.at[s], sh.at[2 * s], rh.at[2 * s], row(-1))
        dn = send(down.at[s], delta.at[s], sh.at[2 * s + 1], rh.at[2 * s + 1], row(1))
        halo += [up, dn]
        head[s] = out[0:edge]
        up.start()
        for c in fifth[s]:
            c.wait_recv()
        ident[0:edge] = eye
        ident[edge:] = jnp.zeros((ident.shape[0] - edge, edge), F32)
        for j in range(inner):
            ops = block(s * blocks_step + j)
            o = offs[0, s, j]
            oe = jnp.minimum(o, REACH)
            x = jnp.concatenate([out[pl.ds(o, tall)], ident[pl.ds(oe, tall)]], 1)
            d = apply(ops, x)
            shift_x[rows - tall : rows] = d[:, :edge]
            shift_e[REACH : REACH + tall] = d[:, edge:]
            for i in range(rows // tall):
                out[i * tall : (i + 1) * tall] -= shift_x[pl.ds(rows - tall - o + i * tall, tall)]
            for i in range(REACH // edge):
                ident[i * edge : (i + 1) * edge] -= shift_e[pl.ds(REACH - oe + i * edge, edge)]
        ops = block(s * blocks_step + inner)
        up.wait_recv()
        x = jnp.concatenate([out[rows - edge :], beneath[s]], 0)
        d = jnp.where(has_below, apply(ops, x), 0.0)
        down[s] = d[edge:]
        dn.start()
        out[rows - edge :] -= d[:edge]
        carry = split(ident[0:REACH])
        dn.wait_recv()
        out[0:REACH] -= mul(carry, split(delta[s]))

    for c in first + second + third + halo:
        c.wait_send()
    for cs in fourth + fifth:
        for c in cs:
            c.wait_send()


def solution(mesh):
    groups = mesh.shape["row"]
    nz = mesh.shape["col"] // NY

    def per_device(vectors, reflectors, wy_factors, block_slots, offsets):
        steps, inner = offsets.shape[1:]
        blocks = steps * (inner + 1)
        rows, width = vectors.shape
        hold, tall, edge = reflectors.shape[1:]
        vr, tr = tall // PIECES, edge // PIECES
        nfar = (nz // T) * (NY // T)
        share = blocks // nfar
        dma = pltpu.SemaphoreType.DMA
        vmem = pltpu.VMEM
        return pl.pallas_call(
            functools.partial(kernel, nz, groups, steps, inner),
            out_shape=jax.ShapeDtypeStruct((rows, width), F32),
            in_specs=[pl.BlockSpec(memory_space=pltpu.SMEM)] * 2 + [pl.BlockSpec(memory_space=pl.ANY)] * 3,
            out_specs=pl.BlockSpec(memory_space=pltpu.VMEM),
            scratch_shapes=[
                vmem((PIECES, hold, vr, edge), F32),
                vmem((PIECES, hold, tr, edge), F32),
                vmem((blocks, vr + tr, edge), F32),
                vmem((nfar, share, vr + tr, edge), F32),
                vmem((blocks, T, T, vr + tr, edge), F32),
                vmem((REACH + tall, width), F32),
                vmem((2 * rows - tall, width), F32),
                vmem((2 * REACH, width), F32),
                vmem((steps, edge, width), F32),
                vmem((steps, edge, width), F32),
                vmem((steps, edge, width), F32),
                vmem((steps, edge, width), F32),
                dma((3,)),
                dma((2 * PIECES,)), dma((2 * PIECES,)),
                dma((nfar,)), dma((nfar,)),
                dma((nfar,)), dma((nfar,)),
                dma((steps * len(NEAR),)), dma((steps * len(NEAR),)),
                dma((steps * len(NEAR),)), dma((steps * len(NEAR),)),
                dma((2 * steps,)), dma((2 * steps,)),
            ],
            compiler_params=pltpu.CompilerParams(
                collective_id=0, has_side_effects=True, vmem_limit_bytes=40 * 1024 * 1024
            ),
        )(block_slots, offsets, vectors, reflectors, wy_factors)

    in_specs = (
        P("row", "col"),
        P("row", "col", None, None),
        P("row", "col", None, None),
        P("row", None, None),
        P("row", None, None),
    )
    return jax.shard_map(per_device, mesh=mesh, in_specs=in_specs, out_specs=P("row", "col"), check_vma=False)
```

time: 915 us -> 112 us (0.12)
  the two profiles are of different devices: /device:TPU:31 before, /device:TPU:16 now
where the time goes in v1:
time: 112 us
  Pallas kernels  107 us (96%)
  local copies, waits for them, and re-layouts  4.83 us (4%)
    pallas_call x1, Pallas kernels, per_device(): pl.pallas_call(functools.partial(kernel, nz, groups, steps, inner), out_s...  107 us
    unnamed x10, local copies, waits for them, and re-layouts  4.83 us

profile of v1, /device:TPU:16, one launch (start us, length us, event | category | flops | bytes accessed | tf_op | source)
XLA Modules:
  0.0 111.8 jit_solution(5471736014219958568)
XLA Ops:
  0.0 0.0 copy-start.3
  0.0 0.8 copy.6.offs
  0.8 0.0 copy-done.3
  0.8 0.0 copy-start
  0.8 1.2 %copy-done = f32[2048,128]{1,0:T(8,128)S(1)} copy-done((f32[2048,128]{1,0:T(8,128)S(1)}, f32[2048,128]{1,0:T(8,128)}, u32[]{:S(2)}) %copy-start) | copy-done | bytes 1048600
  2.0 0.0 copy-start.1
  2.0 0.9 copy-done.1
  3.0 0.0 copy-start.2
  3.0 0.9 copy-done.2
  3.9 106.9 %shard_map.55 = f32[2048,128]{1,0:T(8,128)S(1)} custom-call(s32[1,4,4]{2,1,0:T(4,128)S(1)} %copy-done.3, s32[1,4,3]{2,1,0:T(4,128)S(1)} %copy.6.offs, f32[2048,128]{1,0:T(8,128)S(1)} %copy-done, f32[1,2,256,128]{3,2,1,0:T(8,128)S(1)} %copy-done.1, f32[1,2,128,128]{3,2,1,0:T(8,128)S(1)} %copy-done.2), custom_call_target="tpu_custom_call" | custom-call | tf_op jit(solution)/shard_map/pallas_call | solution.py:246
  110.8 1.0 copy.8
Async XLA Ops:
  0.0 0.8 copy-start.3
  0.8 1.2 %copy-start = (f32[2048,128]{1,0:T(8,128)S(1)}, f32[2048,128]{1,0:T(8,128)}, u32[]{:S(2)}) copy-start(f32[2048,128]{1,0:T(8,128)} %vec.1) | copy-start | bytes 3145732
  2.0 0.9 copy-start.1
  3.0 0.9 copy-start.2

commit v2 on v1

--- a/solution.py
+++ b/solution.py
@@ -14,6 +14,7 @@
 T = 4
 PIECES = T * T
 REACH = 896
+FAR_REACH = 1664
 
 TILE = [(dz, dy) for dz in (-1, 0, 1, 2) for dy in (-1, 0, 1, 2)]
 NEAR = [(1, 0), (-1, 0), (2, 0), (-2, 0), (0, 1), (0, -1), (0, 2), (0, -2)]
@@ -33,14 +34,13 @@
 def kernel(
     nz, groups, steps, inner,
     slots, offs, vec, refl, wy, out,
-    got_v, got_t, mine, far, full, ident, shift_x, shift_e, head, beneath, down, delta,
-    load_sem, s1, r1, s2, r2, s3, r3, s4, r4, s5, r5, sh, rh,
+    got_v, got_t, mine, far, full, ident, pending, shift_x, shift_e, shift_p, head, beneath, down, delta,
+    load_sem, relay, s1, r1, s2, r2, s3, r3, s4, r4, s5, r5, sh, rh,
 ):
     blocks_step = inner + 1
     blocks = steps * blocks_step
     nzh, nyh = nz // T, NY // T
     nfar = nzh * nyh
-    share = blocks // nfar
     group = lax.axis_index("row")
     col = lax.axis_index("col")
     z, y = col // NY, col % NY
@@ -60,19 +60,21 @@
         )
 
     fars = [(a, b) for a in range(nzh) for b in range(nyh) if (a, b) != (0, 0)]
+    fars = sorted(fars, key=lambda ab: (ab[0] == nzh // 2 and ab[1] > 0))
 
     load = pltpu.make_async_copy(vec, out, load_sem.at[0])
     load.start()
 
-    greet = {(-dz, -dy) for dz, dy in TILE} | set(NEAR)
-    greet = {(dz % nz, dy % NY) for dz, dy in greet} | {(T * a, T * b) for a, b in fars}
-    greet = sorted(greet - {(0, 0)})
+    greet = {(-dz, -dy) for dz, dy in TILE} | set(NEAR) | {(T, 0), (-T, 0), (0, T)}
+    greet = sorted({(dz % nz, dy % NY) for dz, dy in greet} - {(0, 0)})
     barrier = pltpu.get_barrier_semaphore()
     for dz, dy in greet:
         pl.semaphore_signal(barrier, inc=1, device_id=at(dz, dy), device_id_type=MESH)
     for d in (1, -1):
         pl.semaphore_signal(barrier, inc=1, device_id=row(d), device_id_type=MESH)
     pl.semaphore_wait(barrier, len(greet) + 2)
+    for i, (dz, dy) in enumerate([(T, 0), (-T, 0), (0, T)]):
+        pl.semaphore_signal(relay.at[i], inc=1, device_id=at(dz, dy), device_id_type=MESH)
 
     first, own = [], []
     vr = got_v.shape[2]
@@ -96,44 +98,56 @@
 
     shift_x[...] = jnp.zeros_like(shift_x)
     shift_e[...] = jnp.zeros_like(shift_e)
+    shift_p[...] = jnp.zeros_like(shift_p)
     for c in own:
         c.wait()
+    for i in range(3):
+        pl.semaphore_wait(relay.at[i], 1)
+    pl.semaphore_signal(relay.at[3], inc=1, device_id=at(0, T), device_id_type=MESH)
     for c in first:
         c.wait_recv()
 
-    for b in range(blocks):
-        slot = slots[0, b // blocks_step, b % blocks_step]
-        root = slot // 2
-        az = (z - root // NY + nz + 1) % nz
-        ay = (y - root % NY + NY + 1) % NY
-        here = jnp.logical_and(az < T, ay < T)
-        k = jnp.minimum(az, T - 1) * T + jnp.minimum(ay, T - 1)
-        half = slot % 2
-        mine[b, 0:vr] = jnp.where(here, got_v[k, half], 0.0)
-        mine[b, vr : vr + tr] = jnp.where(here, got_t[k, half], 0.0)
-    second = []
-    for a, b in fars:
-        k = a * nyh + b
-        dest = ((zh + a) % nzh) * nyh + (yh + b) % nyh
-        second.append(send(mine.at[pl.ds(dest * share, share)], far.at[k], s2.at[k], r2.at[k], at(T * a, T * b)))
-    for c in second:
-        c.start()
-    total = mine[pl.ds(f_me * share, share)]
-    for c in second:
-        c.wait_recv()
-    for k in range(1, nfar):
-        total = total + far[k]
-    full[pl.ds(f_me * share, share), zl, yl] = total
-
-    third = []
-    for a, b in fars:
-        k = a * nyh + b
-        shard = full.at[pl.ds(f_me * share, share), zl, yl]
-        third.append(send(shard, shard, s3.at[k], r3.at[k], at(T * a, T * b)))
-    for c in third:
-        c.start()
-    for c in third:
-        c.wait_recv()
+    lots = blocks // nfar
+    second, third = [], []
+    for lot in range(lots):
+        for b in range(lot * nfar, (lot + 1) * nfar):
+            slot = slots[0, b // blocks_step, b % blocks_step]
+            root = slot // 2
+            az = (z - root // NY + nz + 1) % nz
+            ay = (y - root % NY + NY + 1) % NY
+            here = jnp.logical_and(az < T, ay < T)
+            k = jnp.minimum(az, T - 1) * T + jnp.minimum(ay, T - 1)
+            half = slot % 2
+            mine[b, 0:vr] = jnp.where(here, got_v[k, half], 0.0)
+            mine[b, vr : vr + tr] = jnp.where(here, got_t[k, half], 0.0)
+        sends = []
+        for a, b in fars:
+            k = a * nyh + b
+            dest = lot * nfar + ((zh + a) % nzh) * nyh + (yh + b) % nyh
+            j = lot * nfar + k
+            sends.append(send(mine.at[dest], far.at[lot, k], s2.at[j], r2.at[j], at(T * a, T * b)))
+        for (a, b), c in zip(fars, sends):
+            if lot == 0 and (a, b) == fars[-1]:
+                pl.semaphore_wait(relay.at[3], 1)
+            c.start()
+        second.append(sends)
+
+    for lot in range(lots):
+        me = lot * nfar + f_me
+        total = mine[me]
+        for c in second[lot]:
+            c.wait_recv()
+        for k in range(1, nfar):
+            total = total + far[lot, k]
+        full[me, zl, yl] = total
+        sends = []
+        for a, b in fars:
+            j = lot * nfar + a * nyh + b
+            shard = full.at[me, zl, yl]
+            sends.append(send(shard, shard, s3.at[j], r3.at[j], at(T * a, T * b)))
+        for c in sends:
+            c.start()
+        third.append(sends)
 
     half = blocks_step // 2
 
@@ -161,9 +175,12 @@
 
     fourth = [near(s, 0) for s in range(steps)]
     fifth = [near(s, 1) for s in range(steps)]
-    for cs in fourth:
-        for c in cs:
-            c.start()
+    for lot in range(lots):
+        for c in third[lot]:
+            c.wait_recv()
+        for s in range(lot * steps // lots, (lot + 1) * steps // lots):
+            for c in fourth[s]:
+                c.start()
     load.wait()
     for s in range(steps):
         for c in fourth[s]:
@@ -172,7 +189,7 @@
             c.start()
 
     rows = out.shape[0]
-    edge = head.shape[1]
+    edge = head.shape[2]
     tall = 2 * edge
     has_below = group < groups - 1
     eye = (
@@ -189,12 +206,24 @@
         w = mul(ops[0], split(x))
         return mul(ops[2], split(mul(ops[1], split(w))))
 
+    def place(target, shift, d, o, reach, chunk):
+        start = jnp.minimum(o, reach)
+        shift[reach : reach + tall] = d
+        for i in range(0, reach + (tall if reach + tall == rows else 0), chunk):
+            target[i : i + chunk] -= shift[pl.ds(reach - start + i, chunk)]
+
+    head[0, 0] = out[0:edge]
+    up = send(head.at[0, 0], beneath.at[0, 0], sh.at[0], rh.at[0], row(-1))
+    up.start()
+    ups, dns = [up], []
+    for c in first:
+        c.wait_send()
+    for cs in second + third:
+        for c in cs:
+            c.wait_send()
     for s in range(steps):
-        up = send(head.at[s], beneath.at[s], sh.at[2 * s], rh.at[2 * s], row(-1))
-        dn = send(down.at[s], delta.at[s], sh.at[2 * s + 1], rh.at[2 * s + 1], row(1))
-        halo += [up, dn]
-        head[s] = out[0:edge]
-        up.start()
+        for c in fourth[s] + (fifth[s - 1] if s > 0 else []):
+            c.wait_send()
         for c in fifth[s]:
             c.wait_recv()
         ident[0:edge] = eye
@@ -202,31 +231,42 @@
         for j in range(inner):
             ops = block(s * blocks_step + j)
             o = offs[0, s, j]
-            oe = jnp.minimum(o, REACH)
-            x = jnp.concatenate([out[pl.ds(o, tall)], ident[pl.ds(oe, tall)]], 1)
-            d = apply(ops, x)
-            shift_x[rows - tall : rows] = d[:, :edge]
-            shift_e[REACH : REACH + tall] = d[:, edge:]
-            for i in range(rows // tall):
-                out[i * tall : (i + 1) * tall] -= shift_x[pl.ds(rows - tall - o + i * tall, tall)]
-            for i in range(REACH // edge):
-                ident[i * edge : (i + 1) * edge] -= shift_e[pl.ds(REACH - oe + i * edge, edge)]
+            x = [out[pl.ds(o, tall)], ident[pl.ds(jnp.minimum(o, REACH), tall)]]
+            if s > 0:
+                x.append(pending[pl.ds(jnp.minimum(o, FAR_REACH), tall)])
+            d = apply(ops, jnp.concatenate(x, 1))
+            place(out, shift_x, d[:, :edge], o, rows - tall, tall)
+            place(ident, shift_e, d[:, edge : 2 * edge], o, REACH, edge)
+            if s > 0:
+                place(pending, shift_p, d[:, 2 * edge :], o, FAR_REACH, edge)
+        ups[s].wait_recv()
+        under = beneath[s, 0]
+        if s > 0:
+            under = under - mul(split(beneath[s, 1]), split(down[s - 1]))
         ops = block(s * blocks_step + inner)
-        up.wait_recv()
-        x = jnp.concatenate([out[rows - edge :], beneath[s]], 0)
-        d = jnp.where(has_below, apply(ops, x), 0.0)
+        d = jnp.where(has_below, apply(ops, jnp.concatenate([out[rows - edge :], under], 0)), 0.0)
         down[s] = d[edge:]
+        dn = send(down.at[s], delta.at[s], sh.at[steps + s], rh.at[steps + s], row(1))
         dn.start()
+        dns.append(dn)
         out[rows - edge :] -= d[:edge]
-        carry = split(ident[0:REACH])
-        dn.wait_recv()
-        out[0:REACH] -= mul(carry, split(delta[s]))
-
-    for c in first + second + third + halo:
+        if s > 0:
+            dns[s - 1].wait_recv()
+            out[0:FAR_REACH] -= mul(split(pending[0:FAR_REACH]), split(delta[s - 1]))
+        if s < steps - 1:
+            head[s + 1, 0] = out[0:edge]
+            head[s + 1, 1] = ident[0:edge]
+            up = send(head.at[s + 1], beneath.at[s + 1], sh.at[s + 1], rh.at[s + 1], row(-1))
+            up.start()
+            ups.append(up)
+            pending[0:REACH] = ident[0:REACH]
+            pending[REACH:] = jnp.zeros((pending.shape[0] - REACH, edge), F32)
+    dns[steps - 1].wait_recv()
+    out[0:REACH] -= mul(split(ident[0:REACH]), split(delta[steps - 1]))
+    halo = ups + dns
+
+    for c in fifth[steps - 1] + halo:
         c.wait_send()
-    for cs in fourth + fifth:
-        for c in cs:
-            c.wait_send()
 
 
 def solution(mesh):
@@ -240,7 +280,6 @@
         hold, tall, edge = reflectors.shape[1:]
         vr, tr = tall // PIECES, edge // PIECES
         nfar = (nz // T) * (NY // T)
-        share = blocks // nfar
         dma = pltpu.SemaphoreType.DMA
         vmem = pltpu.VMEM
         return pl.pallas_call(
@@ -252,19 +291,22 @@
                 vmem((PIECES, hold, vr, edge), F32),
                 vmem((PIECES, hold, tr, edge), F32),
                 vmem((blocks, vr + tr, edge), F32),
-                vmem((nfar, share, vr + tr, edge), F32),
+                vmem((blocks // nfar, nfar, vr + tr, edge), F32),
                 vmem((blocks, T, T, vr + tr, edge), F32),
                 vmem((REACH + tall, width), F32),
+                vmem((FAR_REACH + tall, width), F32),
                 vmem((2 * rows - tall, width), F32),
                 vmem((2 * REACH, width), F32),
-                vmem((steps, edge, width), F32),
-                vmem((steps, edge, width), F32),
+                vmem((2 * FAR_REACH, width), F32),
+                vmem((steps, 2, edge, width), F32),
+                vmem((steps, 2, edge, width), F32),
                 vmem((steps, edge, width), F32),
                 vmem((steps, edge, width), F32),
                 dma((3,)),
+                pltpu.SemaphoreType.REGULAR((4,)),
                 dma((2 * PIECES,)), dma((2 * PIECES,)),
-                dma((nfar,)), dma((nfar,)),
-                dma((nfar,)), dma((nfar,)),
+                dma((blocks,)), dma((blocks,)),
+                dma((blocks,)), dma((blocks,)),
                 dma((steps * len(NEAR),)), dma((steps * len(NEAR),)),
                 dma((steps * len(NEAR),)), dma((steps * len(NEAR),)),
                 dma((2 * steps,)), dma((2 * steps,)),

time: 112 us -> 97.7 us (0.87)
  the two profiles are of different devices: /device:TPU:16 before, /device:TPU:64 now
where the time goes in v2:
time: 97.7 us; the launch traced here: 97.4 us
  Pallas kernels  92.6 us (95%)
  local copies, waits for them, and re-layouts  4.83 us (5%)
    pallas_call x1, Pallas kernels, per_device(): pl.pallas_call(functools.partial(kernel, nz, groups, steps, inner), out_s...  92.6 us
    unnamed x10, local copies, waits for them, and re-layouts  4.83 us

profile of v2, /device:TPU:64, one launch (start us, length us, event | category | flops | bytes accessed | tf_op | source)
XLA Modules:
  0.0 97.4 jit_solution(7052600306526867816)
XLA Ops:
  0.0 0.0 copy-start.3
  0.0 0.8 copy.6.offs
  0.8 0.0 copy-done.3
  0.8 0.0 copy-start
  0.8 1.2 %copy-done = f32[2048,128]{1,0:T(8,128)S(1)} copy-done((f32[2048,128]{1,0:T(8,128)S(1)}, f32[2048,128]{1,0:T(8,128)}, u32[]{:S(2)}) %copy-start) | copy-done | bytes 1048600
  2.0 0.0 copy-start.1
  2.0 0.9 copy-done.1
  3.0 0.0 copy-start.2
  3.0 0.9 copy-done.2
  3.9 92.6 %shard_map.55 = f32[2048,128]{1,0:T(8,128)S(1)} custom-call(s32[1,4,4]{2,1,0:T(4,128)S(1)} %copy-done.3, s32[1,4,3]{2,1,0:T(4,128)S(1)} %copy.6.offs, f32[2048,128]{1,0:T(8,128)S(1)} %copy-done, f32[1,2,256,128]{3,2,1,0:T(8,128)S(1)} %copy-done.1, f32[1,2,128,128]{3,2,1,0:T(8,128)S(1)} %copy-done.2), custom_call_target="tpu_custom_call" | custom-call | tf_op jit(solution)/shard_map/pallas_call | solution.py:285
  96.5 1.0 copy.8
Async XLA Ops:
  0.0 0.8 copy-start.3
  0.8 1.2 %copy-start = (f32[2048,128]{1,0:T(8,128)S(1)}, f32[2048,128]{1,0:T(8,128)}, u32[]{:S(2)}) copy-start(f32[2048,128]{1,0:T(8,128)} %vec.1) | copy-start | bytes 3145732
  2.0 0.9 copy-start.1
  3.0 0.9 copy-start.2

commit v3 on v2

v3 whole, which is shorter than its diff:
```python
import functools

import jax
import jax.numpy as jnp
from jax import lax
from jax.experimental import pallas as pl
from jax.experimental.pallas import tpu as pltpu
from jax.sharding import PartitionSpec as P

MESH = pl.DeviceIdType.MESH
F32 = jnp.float32
BF16 = jnp.bfloat16
NY = 8
T = 4
PIECES = T * T
REACH = 896
FAR_REACH = 1664

TILE = [(dz, dy) for dz in (-1, 0, 1, 2) for dy in (-1, 0, 1, 2)]
NEAR = [(1, 0), (-1, 0), (2, 0), (-2, 0), (0, 1), (0, -1), (0, 2), (0, -2)]


def split(x):
    high = x.astype(BF16)
    return high, (x - high.astype(F32)).astype(BF16)


def mul(a, b):
    (ah, al), (bh, bl) = a, b
    dot = functools.partial(jnp.dot, preferred_element_type=F32)
    return dot(ah, bh) + (dot(ah, bl) + dot(al, bh))


def iotas(shape):
    return lax.broadcasted_iota(jnp.int32, shape, 0), lax.broadcasted_iota(jnp.int32, shape, 1)


def pack(basis, factor):
    edge = factor.shape[0]
    mid = edge // 2
    r, c = iotas((edge, edge))
    diag = jnp.where(r == c, factor, 0.0)
    along = jnp.sqrt(jnp.sum(diag, 0, keepdims=True))
    down = jnp.sqrt(jnp.sum(diag, 1, keepdims=True))
    unit = factor / (along * down)
    turned = jnp.concatenate([unit[mid:], jnp.zeros((mid, edge), F32)], 0).T[mid:]
    r, c = iotas((mid, edge))
    return basis * along, jnp.where(jnp.logical_and(c < mid, r > c), turned, unit[:mid])


def unpack(folded):
    mid, edge = folded.shape
    r, c = iotas((mid, edge))
    turned = jnp.concatenate([jnp.zeros((mid, edge), F32), folded], 0).T[:mid]
    top = jnp.where(c > r, folded, jnp.where(c == r, 1.0, 0.0))
    low = jnp.where(c > r + mid, turned, jnp.where(c == r + mid, 1.0, 0.0))
    return jnp.concatenate([top, low], 0)


def kernel(
    nz, groups, steps, inner,
    slots, offs, vec, refl, wy, out,
    base, fold, got_v, got_t, mine, far, far_t, full, ident, pending, shift_x, shift_e, shift_p, head, beneath, down, delta,
    load_sem, relay, s1, r1, s2, r2, s3, r3, st, rt, s4, r4, s5, r5, sh, rh,
):
    blocks_step = inner + 1
    blocks = steps * blocks_step
    nzh, nyh = nz // T, NY // T
    nfar = nzh * nyh
    group = lax.axis_index("row")
    col = lax.axis_index("col")
    z, y = col // NY, col % NY
    zl, yl, zh, yh = z % T, y % T, z // T, y // T
    f_me = zh * nyh + yh
    p_me = zl * T + yl

    def at(dz, dy):
        return {"col": ((z + dz + nz) % nz) * NY + (y + dy + NY) % NY}

    def row(d):
        return {"row": (group + d + groups) % groups}

    def send(src, dst, ssem, rsem, dev):
        return pltpu.make_async_remote_copy(
            src_ref=src, dst_ref=dst, send_sem=ssem, recv_sem=rsem, device_id=dev, device_id_type=MESH
        )

    fars = [(a, b) for a in range(nzh) for b in range(nyh) if (a, b) != (0, 0)]
    fars = sorted(fars, key=lambda ab: (ab[0] == nzh // 2 and ab[1] > 0))

    load = pltpu.make_async_copy(vec, out, load_sem.at[0])
    load.start()

    greet = {(-dz, -dy) for dz, dy in TILE} | set(NEAR) | {(T, 0), (-T, 0), (0, T)}
    greet = sorted({(dz % nz, dy % NY) for dz, dy in greet} - {(0, 0)})
    barrier = pltpu.get_barrier_semaphore()
    for dz, dy in greet:
        pl.semaphore_signal(barrier, inc=1, device_id=at(dz, dy), device_id_type=MESH)
    for d in (1, -1):
        pl.semaphore_signal(barrier, inc=1, device_id=row(d), device_id_type=MESH)
    copies = [
        pltpu.make_async_copy(refl.at[0], base, load_sem.at[1]),
        pltpu.make_async_copy(wy.at[0], fold, load_sem.at[2]),
    ]
    for c in copies:
        c.start()
    for c in copies:
        c.wait()
    mid = fold.shape[1] // 2
    for h in range(base.shape[0]):
        base[h], fold[h, 0:mid] = pack(base[h], fold[h])
    pl.semaphore_wait(barrier, len(greet) + 2)
    for i, (dz, dy) in enumerate([(T, 0), (-T, 0), (0, T)]):
        pl.semaphore_signal(relay.at[i], inc=1, device_id=at(dz, dy), device_id_type=MESH)

    first, own = [], []
    vr = got_v.shape[2]
    tr = got_t.shape[2]
    for k, (dz, dy) in enumerate(TILE):
        p = ((z + dz + nz) % T) * T + (y + dy + NY) % T
        src_v = base.at[:, pl.ds(pl.multiple_of(p * vr, vr), vr)]
        src_t = fold.at[:, pl.ds(pl.multiple_of(p % (PIECES // 2) * tr, tr), tr)]
        if (dz, dy) == (0, 0):
            own = [
                pltpu.make_async_copy(src_v, got_v.at[k], load_sem.at[3]),
                pltpu.make_async_copy(src_t, got_t.at[k], load_sem.at[4]),
            ]
        else:
            first += [
                send(src_v, got_v.at[k], s1.at[k], r1.at[k], at(dz, dy)),
                send(src_t, got_t.at[k], s1.at[k + PIECES], r1.at[k + PIECES], at(dz, dy)),
            ]
    for c in first + own:
        c.start()

    ident[...] = jnp.zeros_like(ident)
    shift_x[...] = jnp.zeros_like(shift_x)
    shift_e[...] = jnp.zeros_like(shift_e)
    shift_p[...] = jnp.zeros_like(shift_p)
    for c in own:
        c.wait()
    for i in range(3):
        pl.semaphore_wait(relay.at[i], 1)
    pl.semaphore_signal(relay.at[3], inc=1, device_id=at(0, T), device_id_type=MESH)
    for c in first:
        c.wait_recv()

    lots = steps
    second, third = [], []
    rest = 2 * vr
    unit = blocks_step * vr // nfar
    units = rest // unit

    def place_of(lot, f):
        return lot * blocks_step // 2 + f // units, pl.ds(pl.multiple_of(f % units * unit, unit), unit)

    def where_is(slot):
        root = slot // 2
        az = (z - root // NY + nz + 1) % nz
        ay = (y - root % NY + NY + 1) % NY
        here = jnp.logical_and(az < T, ay < T)
        return here, jnp.minimum(az, T - 1) * T + jnp.minimum(ay, T - 1), slot % 2

    for lot in range(lots):
        sends = []
        for b in range(lot * blocks_step, (lot + 1) * blocks_step):
            here, k, half = where_is(slots[0, b // blocks_step, b % blocks_step])
            mine[b // 2, (b % 2) * vr : (b % 2 + 1) * vr] = jnp.where(here, got_v[k, half], 0.0)
        if lot == 0:
            for q in range(blocks // 2):
                one = slots[0, 2 * q // blocks_step, 2 * q % blocks_step]
                two = slots[0, (2 * q + 1) // blocks_step, (2 * q + 1) % blocks_step]
                here, k, half = where_is(jnp.where(p_me < PIECES // 2, one, two))
                mine[q, rest : rest + tr] = jnp.where(here, got_t[k, half], 0.0)
        for a, b in fars:
            k = a * nyh + b
            dest = ((zh + a) % nzh) * nyh + (yh + b) % nyh
            q, part = place_of(lot, dest)
            j = lot * nfar + k
            dev = at(T * a, T * b)
            sends.append(send(mine.at[q, part], far.at[lot, k], s2.at[j], r2.at[j], dev))
            if lot == 0:
                src = mine.at[dest, rest : rest + tr]
                sends.append(send(src, far_t.at[k], st.at[k], rt.at[k], dev))
        for i, c in enumerate(sends):
            if lot == 0 and i == 2 * (nfar - 2):
                pl.semaphore_wait(relay.at[3], 1)
            c.start()
        second.append(sends)

    for lot in range(lots):
        me, part = place_of(lot, f_me)
        total = mine[me, part]
        for c in second[lot]:
            c.wait_recv()
        for k in range(1, nfar):
            total = total + far[lot, k]
        full[me, zl, yl, part] = total
        shards = [full.at[me, zl, yl, part]]
        if lot == 0:
            total = mine[f_me, rest : rest + tr]
            for k in range(1, nfar):
                total = total + far_t[k]
            full[f_me, zl, yl, rest : rest + tr] = total
            shards.append(full.at[f_me, zl, yl, rest : rest + tr])
        sends = []
        for a, b in fars:
            k = a * nyh + b
            j = lot * nfar + k
            for i, shard in enumerate(shards):
                ssem, rsem = (s3.at[j], r3.at[j]) if i == 0 else (st.at[nfar + k], rt.at[nfar + k])
                sends.append(send(shard, shard, ssem, rsem, at(T * a, T * b)))
        for c in sends:
            c.start()
        third.append(sends)

    pairs = blocks_step // 2

    def near(step, turn):
        sends = []
        s, r = (s4, r4) if turn == 0 else (s5, r5)
        for i, (dz, dy) in enumerate(NEAR):
            along_z = dy == 0
            lo, n = step * pairs + (0 if along_z == (turn == 0) else pairs // 2), pairs // 2
            rows = slice(0, rest + tr)
            if abs(dz + dy) == 2:
                rows = slice(0, vr) if (dz + dy > 0) == (step % 2 == 0) else slice(vr, rest + tr)
            if turn == 0:
                ref = full.at[pl.ds(lo, n), zl, yl, rows]
            elif along_z:
                ref = full.at[pl.ds(lo, n), zl, :, rows]
            else:
                ref = full.at[pl.ds(lo, n), :, yl, rows]
            j = step * len(NEAR) + i
            sends.append(send(ref, ref, s.at[j], r.at[j], at(dz, dy)))
        return sends

    fourth = [near(s, 0) for s in range(steps)]
    fifth = [near(s, 1) for s in range(steps)]
    for lot in range(lots):
        for c in third[lot]:
            c.wait_recv()
        for s in range(lot * steps // lots, (lot + 1) * steps // lots):
            for c in fourth[s]:
                c.start()
    load.wait()
    for s in range(steps):
        for c in fourth[s]:
            c.wait_recv()
        for c in fifth[s]:
            c.start()

    rows = out.shape[0]
    edge = head.shape[2]
    tall = 2 * edge
    has_below = group < groups - 1
    eye = (
        lax.broadcasted_iota(jnp.int32, (edge, edge), 0) == lax.broadcasted_iota(jnp.int32, (edge, edge), 1)
    ).astype(F32)
    halo = []

    def block(b):
        h = b % 2
        basis = full[b // 2, :, :, h * vr : (h + 1) * vr].reshape(tall, edge)
        factor = unpack(full[b // 2, h * T // 2 : (h + 1) * T // 2, :, rest : rest + tr].reshape(edge // 2, edge))
        return split(basis.T), split(factor), split(basis)

    def apply(ops, x):
        w = mul(ops[0], split(x))
        return mul(ops[2], split(mul(ops[1], split(w))))

    ident[0:edge] = eye

    def window(target, shifts, starts, start, reach, count):
        x = target[pl.ds(start, count)]
        for shift, o in zip(shifts, starts):
            x = x - shift[pl.ds(reach - o + start, count)]
        return x

    head[0, 0] = out[0:edge]
    up = send(head.at[0, 0], beneath.at[0, 0], sh.at[0], rh.at[0], row(-1))
    up.start()
    ups, dns = [up], []
    for c in first:
        c.wait_send()
    for cs in second + third:
        for c in cs:
            c.wait_send()
    for s in range(steps):
        for c in fourth[s] + (fifth[s - 1] if s > 0 else []):
            c.wait_send()
        for c in fifth[s]:
            c.wait_recv()
        at_x, at_e, at_p, parts = [], [], [], []
        for j in range(inner):
            ops = block(s * blocks_step + j)
            o = offs[0, s, j]
            oe, op = jnp.minimum(o, REACH), jnp.minimum(o, FAR_REACH)
            x = [
                window(out, [shift_x.at[i] for i in range(j)], at_x, o, rows - tall, tall),
                window(ident, [shift_e.at[i] for i in range(j)], at_e, oe, REACH, tall),
            ]
            if s > 0:
                x.append(window(pending, [shift_p.at[i] for i in range(j)], at_p, op, FAR_REACH, tall))
            d = apply(ops, jnp.concatenate(x, 1))
            shift_x[j, rows - tall : rows] = d[:, :edge]
            shift_e[j, REACH : REACH + tall] = d[:, edge : 2 * edge]
            if s > 0:
                shift_p[j, FAR_REACH : FAR_REACH + tall] = d[:, 2 * edge :]
            at_x, at_e, at_p = at_x + [o], at_e + [oe], at_p + [op]
        all_x, all_e, all_p = ([f.at[i] for i in range(inner)] for f in (shift_x, shift_e, shift_p))
        ups[s].wait_recv()
        under = beneath[s, 0]
        if s > 0:
            under = under - mul(split(beneath[s, 1]), split(down[s - 1]))
        ops = block(s * blocks_step + inner)
        tail = window(out, all_x, at_x, rows - edge, rows - tall, edge)
        d = jnp.where(has_below, apply(ops, jnp.concatenate([tail, under], 0)), 0.0)
        down[s] = d[edge:]
        dn = send(down.at[s], delta.at[s], sh.at[steps + s], rh.at[steps + s], row(1))
        dn.start()
        dns.append(dn)
        for i in range(0, rows - edge, edge):
            out[i : i + edge] = window(out, all_x, at_x, i, rows - tall, edge)
        out[rows - edge :] = tail - d[:edge]
        if s > 0:
            dns[s - 1].wait_recv()
            coming = split(delta[s - 1])
            carry = window(pending, all_p, at_p, 0, FAR_REACH, FAR_REACH)
            out[0:FAR_REACH] -= mul(split(carry), coming)
        for i in range(0, REACH, edge):
            pending[i : i + edge] = window(ident, all_e, at_e, i, REACH, edge)
        if s == 0:
            pending[REACH:] = jnp.zeros((pending.shape[0] - REACH, edge), F32)
        if s < steps - 1:
            head[s + 1, 0] = out[0:edge]
            head[s + 1, 1] = pending[0:edge]
            up = send(head.at[s + 1], beneath.at[s + 1], sh.at[s + 1], rh.at[s + 1], row(-1))
            up.start()
            ups.append(up)
    dns[steps - 1].wait_recv()
    out[0:REACH] -= mul(split(pending[0:REACH]), split(delta[steps - 1]))
    halo = ups + dns

    for c in fifth[steps - 1] + halo:
        c.wait_send()


def solution(mesh):
    groups = mesh.shape["row"]
    nz = mesh.shape["col"] // NY

    def per_device(vectors, reflectors, wy_factors, block_slots, offsets):
        steps, inner = offsets.shape[1:]
        blocks = steps * (inner + 1)
        rows, width = vectors.shape
        hold, tall, edge = reflectors.shape[1:]
        vr, tr = tall // PIECES, edge // PIECES
        nfar = (nz // T) * (NY // T)
        dma = pltpu.SemaphoreType.DMA
        vmem = pltpu.VMEM
        return pl.pallas_call(
            functools.partial(kernel, nz, groups, steps, inner),
            out_shape=jax.ShapeDtypeStruct((rows, width), F32),
            in_specs=[pl.BlockSpec(memory_space=pltpu.SMEM)] * 2 + [pl.BlockSpec(memory_space=pl.ANY)] * 3,
            out_specs=pl.BlockSpec(memory_space=pltpu.VMEM),
            scratch_shapes=[
                vmem((hold, tall, edge), F32),
                vmem((hold, edge, edge), F32),
                vmem((PIECES, hold, vr, edge), F32),
                vmem((PIECES, hold, tr, edge), F32),
                vmem((blocks // 2, 2 * vr + tr, edge), F32),
                vmem((steps, nfar, (inner + 1) * vr // nfar, edge), F32),
                vmem((nfar, tr, edge), F32),
                vmem((blocks // 2, T, T, 2 * vr + tr, edge), F32),
                vmem((REACH + tall, width), F32),
                vmem((FAR_REACH + tall, width), F32),
                vmem((inner, 2 * rows - tall, width), F32),
                vmem((inner, 2 * REACH + tall, width), F32),
                vmem((inner, 2 * FAR_REACH + tall, width), F32),
                vmem((steps, 2, edge, width), F32),
                vmem((steps, 2, edge, width), F32),
                vmem((steps, edge, width), F32),
                vmem((steps, edge, width), F32),
                dma((5,)),
                pltpu.SemaphoreType.REGULAR((4,)),
                dma((2 * PIECES,)), dma((2 * PIECES,)),
                dma((steps * nfar,)), dma((steps * nfar,)),
                dma((steps * nfar,)), dma((steps * nfar,)),
                dma((2 * nfar,)), dma((2 * nfar,)),
                dma((steps * len(NEAR),)), dma((steps * len(NEAR),)),
                dma((steps * len(NEAR),)), dma((steps * len(NEAR),)),
                dma((2 * steps,)), dma((2 * steps,)),
            ],
            compiler_params=pltpu.CompilerParams(
                collective_id=0, has_side_effects=True, vmem_limit_bytes=40 * 1024 * 1024
            ),
        )(block_slots, offsets, vectors, reflectors, wy_factors)

    in_specs = (
        P("row", "col"),
        P("row", "col", None, None),
        P("row", "col", None, None),
        P("row", None, None),
        P("row", None, None),
    )
    return jax.shard_map(per_device, mesh=mesh, in_specs=in_specs, out_specs=P("row", "col"), check_vma=False)
```

time: 97.7 us -> 95.3 us (0.975)
  the two profiles are of different devices: /device:TPU:64 before, /device:TPU:16 now
where the time goes in v3:
time: 95.3 us; the launch traced here: 95.1 us
  Pallas kernels  90.2 us (95%)
  local copies, waits for them, and re-layouts  4.83 us (5%)
    pallas_call x1, Pallas kernels, per_device(): pl.pallas_call(functools.partial(kernel, nz, groups, steps, inner), out_s...  90.2 us
    unnamed x10, local copies, waits for them, and re-layouts  4.83 us

profile of v3, /device:TPU:16, one launch (start us, length us, event | category | flops | bytes accessed | tf_op | source)
XLA Modules:
  0.0 95.1 jit_solution(1371758286103244133)
XLA Ops:
  0.0 0.0 copy-start.3
  0.0 0.8 copy.6.offs
  0.8 0.0 copy-done.3
  0.8 0.0 copy-start
  0.8 1.2 %copy-done = f32[2048,128]{1,0:T(8,128)S(1)} copy-done((f32[2048,128]{1,0:T(8,128)S(1)}, f32[2048,128]{1,0:T(8,128)}, u32[]{:S(2)}) %copy-start) | copy-done | bytes 1048600
  2.0 0.0 copy-start.1
  2.0 0.9 copy-done.1
  3.0 0.0 copy-start.2
  3.0 0.9 copy-done.2
  3.9 90.2 %shard_map.55 = f32[2048,128]{1,0:T(8,128)S(1)} custom-call(s32[1,4,4]{2,1,0:T(4,128)S(1)} %copy-done.3, s32[1,4,3]{2,1,0:T(4,128)S(1)} %copy.6.offs, f32[2048,128]{1,0:T(8,128)S(1)} %copy-done, f32[1,2,256,128]{3,2,1,0:T(8,128)S(1)} %copy-done.1, f32[1,2,128,128]{3,2,1,0:T(8,128)S(1)} %copy-done.2), custom_call_target="tpu_custom_call" | custom-call | tf_op jit(solution)/shard_map/pallas_call | solution.py:362
  94.1 1.0 %copy.8 = f32[2048,128]{1,0:T(8,128)} copy(f32[2048,128]{1,0:T(8,128)S(1)} %shard_map.55) | data formatting | bytes 2097152
Async XLA Ops:
  0.0 0.8 copy-start.3
  0.8 1.2 %copy-start = (f32[2048,128]{1,0:T(8,128)S(1)}, f32[2048,128]{1,0:T(8,128)}, u32[]{:S(2)}) copy-start(f32[2048,128]{1,0:T(8,128)} %vec.1) | copy-start | bytes 3145732
  2.0 0.9 copy-start.1
  3.0 0.9 copy-start.2

commit v4 on v3

--- a/solution.py
+++ b/solution.py
@@ -309,12 +309,12 @@
                 shift_p[j, FAR_REACH : FAR_REACH + tall] = d[:, 2 * edge :]
             at_x, at_e, at_p = at_x + [o], at_e + [oe], at_p + [op]
         all_x, all_e, all_p = ([f.at[i] for i in range(inner)] for f in (shift_x, shift_e, shift_p))
+        ops = block(s * blocks_step + inner)
+        tail = window(out, all_x, at_x, rows - edge, rows - tall, edge)
         ups[s].wait_recv()
         under = beneath[s, 0]
         if s > 0:
             under = under - mul(split(beneath[s, 1]), split(down[s - 1]))
-        ops = block(s * blocks_step + inner)
-        tail = window(out, all_x, at_x, rows - edge, rows - tall, edge)
         d = jnp.where(has_below, apply(ops, jnp.concatenate([tail, under], 0)), 0.0)
         down[s] = d[edge:]
         dn = send(down.at[s], delta.at[s], sh.at[steps + s], rh.at[steps + s], row(1))
@@ -324,10 +324,9 @@
             out[i : i + edge] = window(out, all_x, at_x, i, rows - tall, edge)
         out[rows - edge :] = tail - d[:edge]
         if s > 0:
+            carry = split(window(pending, all_p, at_p, 0, FAR_REACH, FAR_REACH))
             dns[s - 1].wait_recv()
-            coming = split(delta[s - 1])
-            carry = window(pending, all_p, at_p, 0, FAR_REACH, FAR_REACH)
-            out[0:FAR_REACH] -= mul(split(carry), coming)
+            out[0:FAR_REACH] -= mul(carry, split(delta[s - 1]))
         for i in range(0, REACH, edge):
             pending[i : i + edge] = window(ident, all_e, at_e, i, REACH, edge)
         if s == 0:
@@ -338,8 +337,9 @@
             up = send(head.at[s + 1], beneath.at[s + 1], sh.at[s + 1], rh.at[s + 1], row(-1))
             up.start()
             ups.append(up)
+    carry = split(pending[0:REACH])
     dns[steps - 1].wait_recv()
-    out[0:REACH] -= mul(split(pending[0:REACH]), split(delta[steps - 1]))
+    out[0:REACH] -= mul(carry, split(delta[steps - 1]))
     halo = ups + dns
 
     for c in fifth[steps - 1] + halo:

time: 95.3 us -> 96 us (level)
  no operation moved by 1% of the time
where the time goes in v4:
time: 96 us; the launch traced here: 95.8 us
  Pallas kernels  90.9 us (95%)
  local copies, waits for them, and re-layouts  4.83 us (5%)
    pallas_call x1, Pallas kernels, per_device(): pl.pallas_call(functools.partial(kernel, nz, groups, steps, inner), out_s...  90.9 us
    unnamed x10, local copies, waits for them, and re-layouts  4.83 us

profile of v4, /device:TPU:16, one launch (start us, length us, event | category | flops | bytes accessed | tf_op | source)
XLA Modules:
  0.0 95.8 jit_solution(2754962814950280586)
XLA Ops:
  0.0 0.0 copy-start.3
  0.0 0.8 copy.6.offs
  0.8 0.0 copy-done.3
  0.8 0.0 copy-start
  0.8 1.2 %copy-done = f32[2048,128]{1,0:T(8,128)S(1)} copy-done((f32[2048,128]{1,0:T(8,128)S(1)}, f32[2048,128]{1,0:T(8,128)}, u32[]{:S(2)}) %copy-start) | copy-done | bytes 1048600
  2.0 0.0 copy-start.1
  2.0 0.9 copy-done.1
  3.0 0.0 copy-start.2
  3.0 0.9 copy-done.2
  3.9 90.9 %shard_map.55 = f32[2048,128]{1,0:T(8,128)S(1)} custom-call(s32[1,4,4]{2,1,0:T(4,128)S(1)} %copy-done.3, s32[1,4,3]{2,1,0:T(4,128)S(1)} %copy.6.offs, f32[2048,128]{1,0:T(8,128)S(1)} %copy-done, f32[1,2,256,128]{3,2,1,0:T(8,128)S(1)} %copy-done.1, f32[1,2,128,128]{3,2,1,0:T(8,128)S(1)} %copy-done.2), custom_call_target="tpu_custom_call" | custom-call | tf_op jit(solution)/shard_map/pallas_call | solution.py:362
  94.8 1.0 %copy.8 = f32[2048,128]{1,0:T(8,128)} copy(f32[2048,128]{1,0:T(8,128)S(1)} %shard_map.55) | data formatting | bytes 2097152
Async XLA Ops:
  0.0 0.8 copy-start.3
  0.8 1.2 %copy-start = (f32[2048,128]{1,0:T(8,128)S(1)}, f32[2048,128]{1,0:T(8,128)}, u32[]{:S(2)}) copy-start(f32[2048,128]{1,0:T(8,128)} %vec.1) | copy-start | bytes 3145732
  2.0 0.9 copy-start.1
  3.0 0.9 copy-start.2
